TPU v7x, 128 devices: a whole 4x4x4 slice. The times are simulated.
128 devices in a mesh: row: 8 (over z, core), col: 16 (over y, x).
Axes of the slice: x: 4, y: 4, z: 4, core: 2. Of those that a mesh axis runs over, the one named last changes fastest.
Arguments:
- image_embeds: float32 [32768, 512], P(('row', 'col')), may hold values from -60 to 60
- text_embeds: float32 [32768, 512], P(('col', 'row')), may hold values from -60 to 60
- logit_scale: float32 [], replicated, may hold values from 1 to 4
Outputs:
- grad_image: float32 [32768, 512], P(('row', 'col'))
- grad_text: float32 [32768, 512], P(('col', 'row'))
- grad_scale: float32 [], replicated
All inputs are finite; a program needn't handle non-finite values.
Results may differ from a plain program's by a relative error of at most 0.0023.
The roundings to bfloat16 on the way count: a program that leaves them out, or rounds other values in their place, can miss the bound.
Values may be sent and summed in bfloat16 or wider, within the bound.
A program may use at most 128 MiB of HBM per device.

v0:
```python
import jax
import jax.numpy as jnp
from jax import lax
from jax.sharding import PartitionSpec as P


def on_device(image_embeds, text_embeds, logit_scale):
    image_half = image_embeds.astype(jnp.bfloat16)
    text_half = text_embeds.astype(jnp.bfloat16)
    images = lax.all_gather(image_half, "col", axis=0, tiled=True)
    text_cols = lax.all_gather(text_half, "row", axis=0, tiled=True)
    rows_tile = images.shape[0]
    cols_tile = text_cols.shape[0]
    row_start = lax.axis_index("row") * rows_tile
    col_start = lax.axis_index("col") * cols_tile
    similar = lax.dot_general(
        images, text_cols, (((1,), (1,)), ((), ())), preferred_element_type=jnp.float32
    )
    logits = logit_scale * similar
    row_max = lax.pmax(jnp.max(logits, axis=1), "col")
    col_max = lax.pmax(jnp.max(logits, axis=0), "row")
    row_sum = lax.psum(jnp.sum(jnp.exp(logits - row_max[:, None]), axis=1), "col")
    col_sum = lax.psum(jnp.sum(jnp.exp(logits - col_max[None, :]), axis=0), "row")
    row_lse = row_max + jnp.log(row_sum)
    col_lse = col_max + jnp.log(col_sum)
    row_ids = row_start + jnp.arange(rows_tile, dtype=jnp.int32)
    col_ids = col_start + jnp.arange(cols_tile, dtype=jnp.int32)
    matched = (row_ids[:, None] == col_ids[None, :]).astype(jnp.float32)
    logit_grad = (
        0.5 * jnp.exp(logits - row_lse[:, None])
        + 0.5 * jnp.exp(logits - col_lse[None, :])
        - matched
    )
    partial_scale = jnp.sum(logit_grad * similar)
    grad_half = logit_grad.astype(jnp.bfloat16)
    picked = grad_half
    grad_image = lax.psum_scatter(
        logit_scale * jnp.dot(picked, text_cols, preferred_element_type=jnp.float32),
        "col",
        scatter_dimension=0,
        tiled=True,
    )
    picked = grad_half
    grad_text = lax.psum_scatter(
        logit_scale
        * lax.dot_general(
            picked, images, (((0,), (0,)), ((), ())), preferred_element_type=jnp.float32
        ),
        "row",
        scatter_dimension=0,
        tiled=True,
    )
    grad_scale = lax.psum(partial_scale, ("row", "col"))
    return (grad_image, grad_text, grad_scale)


def solution(mesh):
    placed = (P(("row", "col"), None), P(("col", "row"), None), P())
    return jax.shard_map(
        on_device,
        mesh=mesh,
        in_specs=placed,
        out_specs=(P(("row", "col"), None), P(("col", "row"), None), P()),
        check_vma=False,
    )
```

profile of v0, /device:TPU:0, one launch (start us, length us, event | category | flops | bytes accessed | tf_op | source)
XLA Modules:
  0.0 470.8 jit_solution(6501233213514447022)
XLA Ops:
  7.2 0.0 all-gather.5.cloned.1.call-start
  7.2 1.8 convert_element_type.13
  9.0 0.0 all-gather.5.cloned.1.call-update
  9.0 0.0 all-gather.3.cloned.1.call-start
  9.1 1.8 convert_element_type.12
  10.8 0.0 all-gather.3.cloned.1.call-update
  10.9 0.0 reduce-scatter.5.cloned.1.call-start
  11.6 26.6 %all-gather.5.cloned.1.call-done = bf16[2048,512]{1,0:T(8,128)(2,1)} async-done(((bf16[256,512]{1,0:T(8,128)(2,1)}), bf16[2048,512]{1,0:T(8,128)(2,1)}) %all-gather.5.cloned.1.call-update) | async-done | bytes 2097168 | tf_op jit(solution)/shard_map/all_gather | solution.py:11
  38.2 54.5 %all-gather.3.cloned.1.call-done = bf16[4096,512]{1,0:T(8,128)(2,1)} async-done(((bf16[256,512]{1,0:T(8,128)(2,1)}), bf16[4096,512]{1,0:T(8,128)(2,1)}) %all-gather.3.cloned.1.call-update) | async-done | bytes 4194320 | tf_op jit(solution)/shard_map/all_gather | solution.py:10
  92.7 17.8 %multiply_reduce_fusion.2 = (f32[4096]{0:T(1024)S(1)}, f32[4096,2048]{1,0:T(8,128)}) fusion(f32[]{:T(128)S(6)} %copy.6, bf16[4096,512]{1,0:T(8,128)(2,1)} %all-gather.3.cloned.1.call-done, bf16[2048,512]{1,0:T(8,128)(2,1)} %all-gather.5.cloned.1.call-done), kind=kOutput, calls=%fused_computation.5 | convolution fusion | flops 8606707712 | bytes 39862276 | tf_op jit(solution)/shard_map/dot_general | solution.py:16
  110.5 72.4 %pmax.14 = f32[4096]{0:T(1024)S(1)} all-reduce(f32[4096]{0:T(1024)S(1)} %get-tuple-element.7), channel_id=1, replica_groups=mesh['row'=8,'col'=16] {'col'}, use_global_device_ids=true, to_apply=%region_1.0 | all-reduce | flops 4096 | bytes 32768 | tf_op jit(solution)/shard_map/pmax | solution.py:20
  182.9 14.8 %exponential_reduce_fusion.1 = (f32[4096]{0:T(1024)S(1)}, f32[2048]{0:T(1024)S(1)}) fusion(f32[4096,2048]{1,0:T(8,128)} %get-tuple-element.8, f32[4096]{0:T(1024)S(1)} %pmax.14, f32[]{:T(128)S(6)} %copy.6), kind=kLoop, calls=%fused_computation.3 | loop fusion | flops 33548288 | bytes 33595396 | tf_op jit(solution)/shard_map/reduce_sum | solution.py:22
  197.6 69.5 %psum.21 = f32[4096]{0:T(1024)S(1)} all-reduce(f32[4096]{0:T(1024)S(1)} %get-tuple-element.3), channel_id=1, replica_groups=mesh['row'=8,'col'=16] {'col'}, use_global_device_ids=true, to_apply=%region_3.0 | all-reduce | flops 4096 | bytes 32768 | tf_op jit(solution)/shard_map/psum | solution.py:22
  267.2 12.7 %pmax.15 = f32[2048]{0:T(1024)S(1)} all-reduce(f32[2048]{0:T(1024)S(1)} %get-tuple-element.4), channel_id=1, replica_groups=mesh['row'=8,'col'=16] {'row'}, use_global_device_ids=true, to_apply=%region_5.0 | all-reduce | flops 2048 | bytes 16384 | tf_op jit(solution)/shard_map/pmax | solution.py:21
  279.8 13.8 %exponential_reduce_fusion = f32[2048]{0:T(1024)S(1)} fusion(f32[4096,2048]{1,0:T(8,128)} %get-tuple-element.8, f32[2048]{0:T(1024)S(1)} %pmax.15, f32[]{:T(128)S(6)} %copy.6), kind=kLoop, calls=%fused_computation.2 | loop fusion | flops 25163776 | bytes 33570820 | tf_op jit(solution)/shard_map/reduce_sum | solution.py:23
  293.7 12.8 %psum.22 = f32[2048]{0:T(1024)S(1)} all-reduce(f32[2048]{0:T(1024)S(1)} %exponential_reduce_fusion), channel_id=1, replica_groups=mesh['row'=8,'col'=16] {'row'}, use_global_device_ids=true, to_apply=%region_7.0 | all-reduce | flops 2048 | bytes 16384 | tf_op jit(solution)/shard_map/psum | solution.py:23
  306.5 0.0 copy-start.1
  306.5 0.0 copy-start.2
  306.5 22.0 %multiply_reduce_fusion = (f32[]{:T(128)}, bf16[4096,2048]{1,0:T(8,128)(2,1)S(1)}) fusion(f32[4096,2048]{1,0:T(8,128)} %get-tuple-element.8, s32[2048]{0:T(1024)S(1)} %iota_add_fusion.1, f32[2048]{0:T(1024)S(1)} %log_add_fusion.1, f32[4096]{0:T(1024)S(1)} %log_add_fusion, f32[]{:T(128)S(6)} %copy.6, s32[4096]{0:T(1024)S(1)} %iota_add_fusion), kind=kLoop, calls=%fused_computation | loop fusion | flops 92274688 | bytes 50380808 | tf_op jit(solution)/shard_map/reduce_sum | solution.py:34
  328.5 0.0 copy-start
  328.5 5.7 %copy-done = bf16[4096,2048]{1,0:T(8,128)(2,1)} copy-done((bf16[4096,2048]{1,0:T(8,128)(2,1)}, bf16[4096,2048]{1,0:T(8,128)(2,1)S(1)}, u32[]{:S(2)}) %copy-start) | copy-done | bytes 16777240
  334.3 0.0 copy-done.1
  334.3 10.3 %convolution_multiply_fusion.1 = f32[2048,512]{1,0:T(8,128)} fusion(bf16[4096,2048]{1,0:T(8,128)(2,1)S(1)} %get-tuple-element.6, bf16[4096,512]{1,0:T(8,128)(2,1)S(1)} %copy-done.1, f32[]{:T(128)S(6)} %copy.6), kind=kOutput, calls=%fused_computation.8 | convolution fusion | flops 8590983168 | bytes 25165828 | tf_op jit(solution)/shard_map/dot_general | solution.py:46
  344.6 0.0 reduce-scatter.5.cloned.1.call-update
  344.6 0.0 reduce-scatter.3.cloned.1.call-start
  344.7 0.0 copy-done.2
  344.7 14.8 %convolution_multiply_fusion = f32[4096,512]{1,0:T(8,128)} fusion(bf16[4096,2048]{1,0:T(8,128)(2,1)} %copy-done, bf16[2048,512]{1,0:T(8,128)(2,1)S(1)} %copy-done.2, f32[]{:T(128)S(6)} %copy.6), kind=kOutput, calls=%fused_computation.7 | convolution fusion | flops 8592031744 | bytes 27262980 | tf_op jit(solution)/shard_map/dot_general | solution.py:38
  359.5 0.0 reduce-scatter.3.cloned.1.call-update
  359.5 63.6 %psum.23 = f32[]{:T(128)} all-reduce(f32[]{:T(128)} %get-tuple-element.5), channel_id=1, replica_groups=mesh['row'=8,'col'=16] {'row','col'}, use_global_device_ids=true, to_apply=%region_11.0 | all-reduce | flops 1 | bytes 8 | tf_op jit(solution)/shard_map/psum | solution.py:53
  423.1 0.0 reduce-scatter.5.cloned.1.call-done
  423.1 41.2 %reduce-scatter.3.cloned.1.call-done = f32[256,512]{1,0:T(8,128)} async-done(((f32[4096,512]{1,0:T(8,128)}), f32[256,512]{1,0:T(8,128)}) %reduce-scatter.3.cloned.1.call-update) | async-done | bytes 524304 | tf_op jit(solution)/shard_map/reduce_scatter | solution.py:37
  (4 shorter events, 0.0 us)
Async XLA Ops:
  7.2 31.0 %all-gather.5.cloned.1.call-start = ((), (), s32[]{:S(2)}) async-start(), calls=%async_computation.3 | async-start | bytes 2359296 | tf_op jit(solution)/shard_map/all_gather | solution.py:11
  9.0 83.7 %all-gather.3.cloned.1.call-start = ((), (), s32[]{:S(2)}) async-start(), calls=%async_computation.2 | async-start | bytes 4456448 | tf_op jit(solution)/shard_map/all_gather | solution.py:10
  10.9 412.2 %reduce-scatter.5.cloned.1.call-start = ((), (), s32[]{:S(2)}) async-start(), calls=%async_computation.5 | async-start | bytes 4718592 | tf_op jit(solution)/shard_map/reduce_scatter | solution.py:44
  306.5 27.7 %copy-start.1 = (bf16[4096,512]{1,0:T(8,128)(2,1)S(1)}, bf16[4096,512]{1,0:T(8,128)(2,1)}, u32[]{:S(2)}) copy-start(bf16[4096,512]{1,0:T(8,128)(2,1)} %all-gather.3.cloned.1.call-done) | copy-start | bytes 12582916
  306.5 38.1 %copy-start.2 = (bf16[2048,512]{1,0:T(8,128)(2,1)S(1)}, bf16[2048,512]{1,0:T(8,128)(2,1)}, u32[]{:S(2)}) copy-start(bf16[2048,512]{1,0:T(8,128)(2,1)} %all-gather.5.cloned.1.call-done) | copy-start | bytes 6291460
  328.5 5.7 %copy-start = (bf16[4096,2048]{1,0:T(8,128)(2,1)}, bf16[4096,2048]{1,0:T(8,128)(2,1)S(1)}, u32[]{:S(2)}) copy-start(bf16[4096,2048]{1,0:T(8,128)(2,1)S(1)} %get-tuple-element.6) | copy-start | bytes 50331652
  344.6 119.7 %reduce-scatter.3.cloned.1.call-start = ((), (), s32[]{:S(2)}) async-start(), calls=%async_computation.4 | async-start | bytes 8912896 | tf_op jit(solution)/shard_map/reduce_scatter | solution.py:37
Sparse Core Ops, SparseCore 0:
  10.3 27.8 all-gather.4
  40.9 51.7 all-gather.2
  344.7 31.9 reduce-scatter.4
  380.6 83.6 reduce-scatter.2
where the time goes:
time: 471 us
  blocking collectives  231 us (49%)
  waiting for transfers between devices  122 us (26%)
  other arithmetic  54.1 us (11%)
  matrix products  43 us (9%)
  between operations  14.5 us (3%)
  local copies, waits for them, and re-layouts  5.72 us (1%)
    pmax x1, blocking collectives, on_device(): row_max = lax.pmax(jnp.max(logits, axis=1), 'col')  72.4 us
    psum x1, blocking collectives, on_device(): lax.psum(jnp.sum(jnp.exp(logits - row_max[:, None]), axis=1), 'col')  69.5 us
    psum x1, blocking collectives, on_device(): grad_scale = lax.psum(partial_scale, ('row', 'col'))  63.6 us
    all_gather x1, waiting for transfers between devices, on_device(): images = lax.all_gather(image_half, 'col', axis=0, tiled=True)  54.5 us
    reduce_scatter x1, waiting for transfers between devices, on_device(): lax.psum_scatter(logit_scale * jnp.dot(picked, text_cols, preferred_eleme...  41.2 us
    all_gather x1, waiting for transfers between devices, on_device(): text_cols = lax.all_gather(text_half, 'row', axis=0, tiled=True)  26.6 us
    reduce_sum x1, other arithmetic, on_device(): partial_scale = jnp.sum(logit_grad * similar)  22 us
    dot_general x1, matrix products, on_device(): lax.dot_general(images, text_cols, (((1,), (1,)), ((), ())), preferred_el...  17.8 us
  transfers between devices with their start and end apart: 4, of which 3 were waited for; matrix products, arithmetic and copies ran while one was open for 4% of the time, Pallas kernels for 0%

commit v1 on v0

v1 whole, which is shorter than its diff:
```python
import functools

import jax
import jax.numpy as jnp
from jax import lax
from jax.experimental import pallas as pl
from jax.experimental.pallas import tpu as pltpu
from jax.sharding import PartitionSpec as P

MESH = pl.DeviceIdType.MESH
NT = (((1,), (1,)), ((), ()))
TN = (((0,), (0,)), ((), ()))
LOG2E = 1.4426950408889634
B = 256
E = 512
H = B // 2
KEPT = 6

IMG = ((0, 0), (0, 1), (1, 0), (3, 0), (2, 0), (1, 1), (3, 1), (2, 1))
TXT = ((0, 0), (0, 1), (1, 0), (3, 0), (1, 1), (3, 1), (2, 0), (2, 1))
TEXT_ORDER = (7, 5, 4, 6, 3, 2, 1, 0)

GI, GT, SIB, RI, RT, DD = 0, 14, 28, 36, 49, 62
ROWS, COLS, SC1, SC2, CHANNELS = 70, 86, 94, 110, 118


def look_up(i, values):
    return sum(v * (i == n).astype(jnp.int32) for n, v in enumerate(values) if v)


def slot_ring(i, slots):
    return look_up(i, [d for d, _ in slots])


def slot_pair(i, slots):
    return look_up(i, [d for _, d in slots])


def text_slot(ring, pair):
    return sum(
        s * ((ring == d) & (pair == e)).astype(jnp.int32)
        for s, (d, e) in enumerate(TXT)
        if s
    )


def kernel(
    scale_ref, img_hbm, txt_hbm, gi_hbm, gt_hbm, gs_ref,
    I, T, LE, LO, TME, TMO, CME, CMO, GE, GO, MS, PB, XS, FR, XR, AR, FRT, XRT, ART,
    MC, SC, RSEND, RRECV, CSEND, CRECV, RLSE, CLSE, ACC, SR1, SR2,
    SS, RS, LS,
):
    f32, bf16 = jnp.float32, jnp.bfloat16
    r, c = lax.axis_index("row"), lax.axis_index("col")
    z, k = r // 2, r % 2
    y, x = c // 4, c % 4
    b = y // 2
    a = (y + b) % 2
    L, TM, CM, G = (LE, LO), (TME, TMO), (CME, CMO), (GE, GO)

    def dev(dx=0, da=0, dk=0, dz=0, db=0):
        xx, zz, kk = (x + dx) % 4, (z + dz) % 4, (k + dk) % 2
        aa, bb = (a + da) % 2, (b + db) % 2
        yy = aa + bb * (3 - 2 * aa)
        return (zz * 2 + kk, yy * 4 + xx)

    def chan(n, src, dst, to):
        return pltpu.make_async_remote_copy(
            src_ref=src, dst_ref=dst, send_sem=SS.at[n], recv_sem=RS.at[n],
            device_id=to, device_id_type=MESH,
        )

    row_peers = [(dx, da, dk) for dk in (0, 1) for da in (0, 1) for dx in range(4) if (dx, da, dk) != (0, 0, 0)]
    col_peers = [(dz, db) for db in (0, 1) for dz in range(4) if (dz, db) != (0, 0)]

    load_i = pltpu.make_async_copy(img_hbm, LE.at[0:B, 0:E], LS.at[0])
    load_t = pltpu.make_async_copy(txt_hbm, LO.at[0:B, 0:E], LS.at[1])
    load_i.start()
    load_t.start()

    barrier = pltpu.get_barrier_semaphore()
    near = [dev(dx=1), dev(dx=3), dev(da=1), dev(dz=1), dev(dz=3), dev(db=1), dev(dk=1)]
    for to in near:
        pl.semaphore_signal(barrier, inc=1, device_id=to, device_id_type=MESH)

    scale = scale_ref[0]
    c2 = scale * LOG2E
    load_i.wait()
    I[0:B, :] = LE[0:B, 0:E].astype(bf16)
    load_t.wait()
    T[0:B, :] = LO[0:B, 0:E].astype(bf16)
    MC[...] = jnp.full(MC.shape, -1e30, f32)
    SC[...] = jnp.zeros(SC.shape, f32)
    MS[:, :, 0:B] = jnp.full((8, B, B), -1e30, f32)
    MS[:, :, B : 2 * B] = jnp.zeros((8, B, B), f32)
    ACC[...] = jnp.zeros(ACC.shape, f32)
    pl.semaphore_wait(barrier, len(near))

    def gather(base, buf, step, slots, plus, minus, partner):
        def at(place, h):
            lo = slots.index(place) * step * B + h * H
            return buf.at[lo : lo + H]

        plan = [
            ("own", (0, 0), partner, (0, 1), (0, 1)),
            ("own", (0, 0), plus, (3, 0), (0, 1)),
            ("own", (0, 0), minus, (1, 0), (1, 0)),
            ("pair", (0, 1), plus, (3, 1), (0, 1)),
            ("pair", (0, 1), minus, (1, 1), (1, 0)),
            ("on", (3, 0), plus, (2, 0), (0,)),
            ("on", (1, 0), minus, (2, 0), (1,)),
            ("on", (3, 1), plus, (2, 1), (0,)),
            ("on", (1, 1), minus, (2, 1), (1,)),
        ]
        out, n = {}, base
        for _, src, to, dst, halves in plan:
            for h in halves:
                out[dst, h, src] = chan(n, at(src, h), at(dst, h), to)
                n += 1
        return out

    xp, xm, pa = dev(dx=1), dev(dx=3), dev(da=1)
    zp, zm, pb = dev(dz=1), dev(dz=3), dev(db=1)
    sib = dev(dk=1)
    gi = gather(GI, I, 2, IMG, xp, xm, pa)
    gt = gather(GT, T, 1, TXT, zp, zm, pb)
    sb = {
        p: chan(SIB + s, I.at[2 * s * B : (2 * s + 1) * B], I.at[(2 * s + 1) * B : (2 * s + 2) * B], sib)
        for s, p in enumerate(IMG)
    }

    def come(cps, dst, h):
        for (to, half, _), cp in cps.items():
            if (to, half) == (dst, h):
                cp.wait_recv()

    for first in (True, False):
        for dst, hh in (((0, 1), (0, 1)), ((3, 0), (0, 1)), ((1, 0), (1, 0))):
            h = hh[0] if first else hh[1]
            gi[dst, h, (0, 0)].start()
            gt[dst, h, (0, 0)].start()
    sb[0, 0].start()

    def logit_tile(i, jp, e):
        xt = lax.dot_general(
            I[pl.ds(pl.multiple_of(i * 2 * B, 2 * B), 2 * B), :],
            T[pl.ds(pl.multiple_of(jp * 2 * B + e * B, B), B), :],
            NT, preferred_element_type=f32,
        )
        return xt * c2

    def lrow(i):
        return pl.multiple_of(jnp.minimum(i, KEPT - 1) * 2 * B, 2 * B)

    def mm_section(i, jp, e):
        xt = logit_tile(i, jp, e)
        L[e][pl.ds(lrow(i), 2 * B), pl.ds(pl.multiple_of(jp * B, B), B)] = xt
        TM[e][...] = jnp.maximum(xt[:, :128], xt[:, 128:])
        CM[e][...] = jnp.max(xt.reshape(2 * B // 8, 8, B), axis=0)

    def st_section(i, jp, e):
        cols = pl.ds(pl.multiple_of(jp * 2 * B + e * B, B), B)
        old = MC[:, cols]
        mc = jnp.maximum(old, CM[e][...])
        MC[:, cols] = mc
        acc = SC[:, cols] * jnp.exp2(old - mc)
        U = 64
        for q in (0, 1):
            for u in range(B // U):
                l = L[e][pl.ds(lrow(i) + q * B + u * U, U), pl.ds(pl.multiple_of(jp * B, B), B)]
                rows, mcol, scol = slice(u * U, (u + 1) * U), slice(q * 128, (q + 1) * 128), slice(B + q * 128, B + (q + 1) * 128)
                old = MS[i, rows, mcol]
                m = jnp.maximum(old, TM[e][q * B + u * U : q * B + (u + 1) * U])
                MS[i, rows, mcol] = m
                MS[i, rows, scol] = (
                    MS[i, rows, scol] * jnp.exp2(old - m) + jnp.exp2(l[:, :128] - m) + jnp.exp2(l[:, 128:] - m)
                )
                acc = acc + jnp.sum(jnp.exp2(l.reshape(U // 8, 8, B) - mc[None]), axis=0)
        SC[:, cols] = acc

    def body(i, jp, prev):
        st_section(prev[0], prev[1], 1)
        mm_section(i, jp, 0)
        st_section(i, jp, 0)
        mm_section(i, jp, 1)
        return (i, jp)

    def sweep(n, index, prev):
        def one(t, carry):
            i, jp = index(t)
            return body(i, jp, carry)

        return lax.fori_loop(0, n, one, prev)

    for cps in (gi, gt):
        come(cps, (0, 1), 0)
        cps[(3, 1), 0, (0, 1)].start()
    for cps in (gi, gt):
        come(cps, (0, 1), 1)
        cps[(1, 1), 1, (0, 1)].start()
        cps[(3, 1), 1, (0, 1)].start()
        cps[(1, 1), 0, (0, 1)].start()
    for cps in (gi, gt):
        come(cps, (3, 0), 0)
        cps[(2, 0), 0, (3, 0)].start()
        come(cps, (1, 0), 1)
        cps[(2, 0), 1, (1, 0)].start()
    sb[0, 1].start()
    for cps in (gi, gt):
        come(cps, (3, 0), 1)
        come(cps, (1, 0), 0)
    sb[3, 0].start()
    sb[1, 0].start()
    for p in ((0, 0), (0, 1), (3, 0), (1, 0)):
        sb[p].wait_recv()

    zero = jnp.int32(0)
    mm_section(zero, zero, 0)
    st_section(zero, zero, 0)
    mm_section(zero, zero, 1)
    prev = (zero, zero)
    prev = sweep(7, lambda t: ((t + 1) // 2, (t + 1) % 2), prev)

    for cps in (gi, gt):
        come(cps, (3, 1), 0)
        cps[(2, 1), 0, (3, 1)].start()
        come(cps, (1, 1), 1)
        cps[(2, 1), 1, (1, 1)].start()
    for cps in (gi, gt):
        come(cps, (3, 1), 1)
        come(cps, (1, 1), 0)
    sb[3, 1].start()
    sb[1, 1].start()
    prev = sweep(4, lambda t: (t, zero + 2), prev)
    sb[3, 1].wait_recv()
    sb[1, 1].wait_recv()
    prev = sweep(6, lambda t: (5 + t // 3, t % 3), prev)

    come(gi, (2, 0), 0)
    come(gi, (2, 0), 1)
    sb[2, 0].start()
    sb[2, 0].wait_recv()
    prev = sweep(3, lambda t: (zero + 4, t), prev)
    for p in ((2, 0), (2, 1)):
        for h in (0, 1):
            come(gt, p, h)
    come(gi, (2, 1), 0)
    come(gi, (2, 1), 1)
    sb[2, 1].start()
    prev = sweep(7, lambda t: (t, zero + 3), prev)
    sb[2, 1].wait_recv()
    prev = sweep(4, lambda t: (zero + 7, t), prev)
    st_section(prev[0], prev[1], 1)

    eye = lax.broadcasted_iota(jnp.int32, (128, 128), 0) == lax.broadcasted_iota(jnp.int32, (128, 128), 1)

    def image_block(i, q):
        return ((k + q) % 2) * 8 + ((a + slot_pair(i, IMG)) % 2) * 4 + (x + slot_ring(i, IMG)) % 4

    def text_block(j):
        return ((b + slot_pair(j, TXT)) % 2) * 4 + (z + slot_ring(j, TXT)) % 4

    def row_lse(i, carry):
        for q in (0, 1):
            m = MS[i, :, q * 128 : (q + 1) * 128]
            s = MS[i, :, B + q * 128 : B + (q + 1) * 128]
            mr = jnp.max(m, axis=1, keepdims=True)
            lse = mr + jnp.log2(jnp.sum(s * jnp.exp2(m - mr), axis=1, keepdims=True))
            for h in (0, 1):
                v = jnp.broadcast_to(lse[h * 128 : (h + 1) * 128], (128, 128))
                RSEND[pl.ds(image_block(i, q) * 2 + h, 1), :] = jnp.sum(jnp.where(eye, v, 0.0), axis=0, keepdims=True)
        return carry

    lax.fori_loop(0, 8, row_lse, 0)
    rows_out = []
    for dx, da, dk in row_peers:
        to, here = dk * 8 + da * 4 + dx, dk * 8 + da * 4 + (4 - dx) % 4
        rows_out.append(chan(ROWS + here, RSEND, RRECV.at[here], dev(dx=dx, da=da, dk=dk)))
        rows_out[-1].start()
    mc = MC[...]
    mr = jnp.max(mc, axis=0, keepdims=True)
    lse = mr + jnp.log2(jnp.sum(SC[...] * jnp.exp2(mc - mr), axis=0, keepdims=True))
    for j in range(8):
        for h in (0, 1):
            CSEND[pl.ds(text_block(jnp.int32(j)) * 2 + h, 1), :] = lse[:, j * B + h * 128 : j * B + (h + 1) * 128]
    cols_out = []
    for dz, db in col_peers:
        here = db * 4 + (4 - dz) % 4
        cols_out.append(chan(COLS + here, CSEND, CRECV.at[here], dev(dz=dz, db=db)))
        cols_out[-1].start()

    for cp in cols_out:
        cp.wait_recv()
    parts = [CSEND[...]] + [CRECV[n] for n in range(1, 8)]
    m = functools.reduce(jnp.maximum, parts)
    CLSE[...] = m + 1.0 + jnp.log2(sum(jnp.exp2(v - m) for v in parts))
    for j in range(8):
        for h in (0, 1):
            MC[:, j * B + h * 128 : j * B + (h + 1) * 128] = jnp.broadcast_to(
                CLSE[pl.ds(text_block(jnp.int32(j)) * 2 + h, 1), :], (8, 128)
            )
    for cp in rows_out:
        cp.wait_recv()
    parts = [RSEND[...]] + [RRECV[n] for n in range(1, 16)]
    m = functools.reduce(jnp.maximum, parts)
    RLSE[...] = m + 1.0 + jnp.log2(sum(jnp.exp2(v - m) for v in parts))

    for cp in [*gi.values(), *gt.values(), *sb.values()]:
        cp.wait_send()

    def row_col(i, q, h):
        v = RLSE[pl.ds(image_block(i, q) * 2 + h, 1), :]
        v = jnp.sum(jnp.where(eye, jnp.broadcast_to(v, (128, 128)), 0.0), axis=1, keepdims=True)
        return jnp.broadcast_to(v, (128, 128))

    def grow(i):
        return pl.multiple_of((i // 2) * 2 * B, 2 * B)

    def grads(i, e):
        U = 32
        acc = ACC[...]
        for q in (0, 1):
            for h in (0, 1):
                rl = row_col(i, q, h)
                for u in range(128 // U):
                    off = q * B + h * 128 + u * U
                    rb = rl[u * U : (u + 1) * U]
                    rb = jnp.concatenate([rb, rb], axis=1)
                    for j in range(8):
                        l = L[j % 2][pl.ds(lrow(i) + off, U), (j // 2) * B : (j // 2 + 1) * B]
                        cl = MC[:, j * B : (j + 1) * B]
                        g = jnp.exp2(l - rb) + jnp.exp2(l.reshape(U // 8, 8, B) - cl[None]).reshape(U, B)
                        w = jnp.sum((g * l).reshape(U // 8, 8, B), axis=0)
                        acc = acc + w[:, :128] + w[:, 128:]
                        G[e][pl.ds(grow(i) + off, U), j * B : (j + 1) * B] = g.astype(bf16)
        ACC[...] = acc

    def matched(i, par):
        ai, xi = (a + slot_pair(i, IMG)) % 2, (x + slot_ring(i, IMG)) % 4
        yi = ai + b * (3 - 2 * ai)
        here = (x % 2 == b) & ((z + z // 2) % 2 == a) & (xi % 2 == k)
        j = text_slot((2 * (yi % 2) + xi // 2 - z + 4) % 4, (z // 2 + b) % 2)
        for q in (0, 1):
            for e in (0, 1):

                @pl.when(here & ((k + q) % 2 == x // 2) & (j % 2 == e))
                def _():
                    for h in (0, 1):
                        rows = q * B + h * 128
                        l = L[e][pl.ds(lrow(i) + rows, 128), pl.ds(pl.multiple_of((j // 2) * B + h * 128, 128), 128)]
                        cl = MC[0:1, pl.ds(pl.multiple_of(j * B + h * 128, 128), 128)]
                        g = jnp.exp2(l - row_col(i, q, h)) + jnp.exp2(l - cl)
                        g = jnp.where(eye, g - 1.0, g)
                        G[par][
                            pl.ds(grow(i) + rows, 128),
                            pl.ds(pl.multiple_of(j * B + h * 128, 128), 128),
                        ] = g.astype(bf16)
                        w = jnp.where(eye, l, 0.0)
                        ACC[...] -= jnp.sum(w.reshape(16, 8, 128), axis=0)

    def image_product(i, e):
        p = jnp.dot(G[e][pl.ds(grow(i), 2 * B), :], T[...], preferred_element_type=f32)
        PB[e, 0] = p[:B]
        PB[e, 1] = p[B:]

    def scatter(base, src, own, fr, xr, ar, plus, minus, partner):
        out = {}
        for n, p in enumerate((1, 0)):
            s, lo, hi = base + 6 * n, slice(0, H), slice(H, B)
            out[2, p, 0] = chan(s + 0, src((2, p)).at[lo], fr.at[p, 0], plus)
            out[2, p, 1] = chan(s + 1, src((2, p)).at[hi], fr.at[p, 1], minus)
            out[1, p, 0] = chan(s + 2, src((1, p)).at[lo], xr.at[0, p, lo], plus)
            out[1, p, 1] = chan(s + 3, src((1, p)).at[hi], xr.at[0, p, hi], plus)
            out[3, p, 0] = chan(s + 4, src((3, p)).at[lo], xr.at[1, p, lo], minus)
            out[3, p, 1] = chan(s + 5, src((3, p)).at[hi], xr.at[1, p, hi], minus)
        out[0, 1] = chan(base + 12, own, ar, partner)
        return out

    stage = {(2, 1): 0, (3, 1): 1, (1, 1): 2, (2, 0): 3, (3, 0): 0, (1, 0): 1}
    xs = lambda place: XS.at[stage[place]]
    ts = lambda place: T.at[TXT.index(place) * B : (TXT.index(place) + 1) * B]
    ltext = lambda s: LE.at[s * B : (s + 1) * B, 0:E]
    ri = scatter(RI, xs, MS.at[1], FR, XR, AR, xp, xm, pa)
    rt = scatter(RT, ts, ltext(1), FRT, XRT, ART, zp, zm, pb)

    def across(i, e):
        return chan(DD + i, PB.at[e, 1], MS.at[i], sib)

    def half(h):
        return pl.ds(h * H, H)

    def send_far(cps, place, p, stage_ref):
        stage_ref[...] = p[...].astype(bf16)
        cps[(*place, 0)].start()
        cps[(*place, 1)].start()

    mixed = {1: 0, 3: 1}

    def send_pure(cps, place, p, stage_ref):
        h = 1 - mixed[place[0]]
        stage_ref[half(h)] = p[half(h)].astype(bf16)
        cps[(*place, h)].start()

    def send_mixed(cps, place, p, stage_ref, fr):
        h = mixed[place[0]]
        cps[2, place[1], h].wait_recv()
        stage_ref[half(h)] = (p[half(h)] + fr[place[1], h].astype(f32)).astype(bf16)
        cps[(*place, h)].start()

    def arrived(cps, pair):
        for ring in (1, 3):
            for h in (0, 1):
                cps[ring, pair, h].wait_recv()

    def send_pair(cps, p, xr):
        arrived(cps, 1)
        p[...] += xr[0, 1].astype(f32) + xr[1, 1].astype(f32)
        cps[0, 1].start()

    frees = {(3, 0): (2, 1), (1, 0): (3, 1)}
    waited = [(*frees[p], h) for p in frees for h in (0, 1)]

    def image_sum(s):
        place = IMG[s]
        across(s, s % 2).wait_recv()
        MS[s] += PB[s % 2, 0]
        if place in frees:
            for h in (0, 1):
                ri[(*frees[place], h)].wait_send()
        if place[0] == 2:
            send_far(ri, place, MS.at[s], xs(place))
        elif place[0]:
            send_pure(ri, place, MS.at[s], xs(place))
        across(s, s % 2).wait_send()

    def image_mixed(place):
        send_mixed(ri, place, MS.at[IMG.index(place)], xs(place), FR)

    def again(i):
        @pl.when((i >= KEPT - 1) & (i < 7))
        def _():
            for e in (0, 1):
                for jp in range(4):
                    L[e][(KEPT - 1) * 2 * B : KEPT * 2 * B, jp * B : (jp + 1) * B] = logit_tile(i, jp, e)

    def g_half(i, e):
        again(i)
        grads(i, e)
        image_product(i + 1, 1 - e)
        matched(i, e)
        across(i + 1, 1 - e).start()
        for s in range(7, 1, -1):
            if s % 2 == e:

                @pl.when(i + 2 == s)
                def _():
                    image_sum(s)

    def g_step(t, carry):
        g_half(6 - 2 * t, 0)

        @pl.when(t == 2)
        def _():
            image_mixed((3, 1))
            image_mixed((1, 1))

        g_half(5 - 2 * t, 1)
        return carry

    seven = jnp.int32(7)
    grads(seven, 1)
    matched(seven, 1)
    lax.fori_loop(0, 3, g_step, 0)
    g_half(zero, 0)

    sc1_out = []
    mine = image_block(zero, 0)
    SR1[mine] = ACC[...]
    for dx, da, dk in row_peers:
        here = dk * 8 + da * 4 + (4 - dx) % 4
        sc1_out.append(chan(SC1 + here, ACC, SR1.at[mine], dev(dx=dx, da=da, dk=dk)))
        sc1_out[-1].start()

    image_product(zero, 0)
    across(zero, 0).start()

    mine_t = text_block(zero)
    sc2_out = [
        chan(SC2 + db * 4 + (4 - dz) % 4, ACC, SR2.at[mine_t], dev(dz=dz, db=db)) for dz, db in col_peers
    ]

    def text_send(kind, place, *more):
        kind(rt, place, ltext(TXT.index(place)), ts(place), *more)

    def text_step(t, carry):
        j = look_up(t, TEXT_ORDER)
        cols = pl.ds(pl.multiple_of(j * B, B), B)
        p = None
        for s in range(8):
            v = lax.dot_general(
                G[s % 2][(s // 2) * 2 * B : (s // 2 + 1) * 2 * B, cols],
                I[s * 2 * B : (s + 1) * 2 * B, :],
                TN, preferred_element_type=f32,
            )
            p = v if p is None else p + v
        LE[pl.ds(pl.multiple_of(j * B, B), B), 0:E] = p

        @pl.when(t == 0)
        def _():
            text_send(send_far, (2, 1))
            image_sum(1)
            image_sum(0)
            image_mixed((3, 0))
            image_mixed((1, 0))

        @pl.when(t == 1)
        def _():
            text_send(send_pure, (3, 1))

        @pl.when(t == 2)
        def _():
            text_send(send_pure, (1, 1))

        @pl.when(t == 3)
        def _():
            text_send(send_mixed, (3, 1), FRT)
            text_send(send_mixed, (1, 1), FRT)
            text_send(send_far, (2, 0))

        @pl.when(t == 4)
        def _():
            text_send(send_pure, (3, 0))
            send_pair(ri, MS.at[1], XR)

        @pl.when(t == 5)
        def _():
            text_send(send_pure, (1, 0))
            for cp in sc1_out:
                cp.wait()
            ACC[...] = sum(SR1[n] for n in range(16))
            SR2[mine_t] = ACC[...]
            for cp in sc2_out:
                cp.start()

        @pl.when(t == 7)
        def _():
            text_send(send_mixed, (3, 0), FRT)
            text_send(send_mixed, (1, 0), FRT)

        return carry

    lax.fori_loop(0, 8, text_step, 0)

    def finish(cps, p, xr, ar, out, sem):
        arrived(cps, 0)
        p[...] += xr[0, 0].astype(f32) + xr[1, 0].astype(f32)
        cps[0, 1].wait_recv()
        p[...] = scale * (p[...] + ar[...])
        store = pltpu.make_async_copy(p, out, sem)
        store.start()
        return store

    send_pair(rt, ltext(1), XRT)
    for cp in sc2_out:
        cp.wait()
    gs_ref[0, 0] = jnp.sum(sum(SR2[n] for n in range(8))) / c2
    store_i = finish(ri, MS.at[0], XR, AR, gi_hbm, LS.at[0])
    store_t = finish(rt, ltext(0), XRT, ART, gt_hbm, LS.at[1])

    for cp in rows_out + cols_out:
        cp.wait_send()
    for name, cp in ri.items():
        if name not in waited:
            cp.wait_send()
    for cp in rt.values():
        cp.wait_send()
    store_i.wait()
    store_t.wait()


def on_device(image_embeds, text_embeds, logit_scale):
    f32, bf16 = jnp.float32, jnp.bfloat16
    any_space = pl.BlockSpec(memory_space=pl.ANY)
    smem = pl.BlockSpec(memory_space=pltpu.SMEM)
    grad_image, grad_text, grad_scale = pl.pallas_call(
        kernel,
        out_shape=(
            jax.ShapeDtypeStruct((B, E), f32),
            jax.ShapeDtypeStruct((B, E), f32),
            jax.ShapeDtypeStruct((1, 1), f32),
        ),
        in_specs=[smem, any_space, any_space],
        out_specs=(any_space, any_space, smem),
        scratch_shapes=[
            pltpu.VMEM((16 * B, E), bf16),
            pltpu.VMEM((8 * B, E), bf16),
            pltpu.VMEM((KEPT * 2 * B, 4 * B), f32),
            pltpu.VMEM((KEPT * 2 * B, 4 * B), f32),
            pltpu.VMEM((2 * B, 128), f32),
            pltpu.VMEM((2 * B, 128), f32),
            pltpu.VMEM((8, B), f32),
            pltpu.VMEM((8, B), f32),
            pltpu.VMEM((8 * B, 8 * B), bf16),
            pltpu.VMEM((8 * B, 8 * B), bf16),
            pltpu.VMEM((8, B, E), f32),
            pltpu.VMEM((2, 2, B, E), f32),
            pltpu.VMEM((4, B, E), bf16),
            pltpu.VMEM((2, 2, H, E), bf16),
            pltpu.VMEM((2, 2, B, E), bf16),
            pltpu.VMEM((B, E), f32),
            pltpu.VMEM((2, 2, H, E), bf16),
            pltpu.VMEM((2, 2, B, E), bf16),
            pltpu.VMEM((B, E), f32),
            pltpu.VMEM((8, 8 * B), f32),
            pltpu.VMEM((8, 8 * B), f32),
            pltpu.VMEM((32, 128), f32),
            pltpu.VMEM((16, 32, 128), f32),
            pltpu.VMEM((16, 128), f32),
            pltpu.VMEM((8, 16, 128), f32),
            pltpu.VMEM((32, 128), f32),
            pltpu.VMEM((16, 128), f32),
            pltpu.VMEM((8, 128), f32),
            pltpu.VMEM((16, 8, 128), f32),
            pltpu.VMEM((8, 8, 128), f32),
            pltpu.SemaphoreType.DMA((CHANNELS,)),
            pltpu.SemaphoreType.DMA((CHANNELS,)),
            pltpu.SemaphoreType.DMA((2,)),
        ],
        compiler_params=pltpu.CompilerParams(
            collective_id=0, has_side_effects=True, vmem_limit_bytes=64 << 20
        ),
        cost_estimate=pl.CostEstimate(flops=6 * 4096 * 2048 * 512, bytes_accessed=4 << 20, transcendentals=4 * 4096 * 2048),
    )(logit_scale.reshape(1), image_embeds, text_embeds)
    return grad_image, grad_text, grad_scale.reshape(())


def solution(mesh):
    return jax.shard_map(
        on_device,
        mesh=mesh,
        in_specs=(P(("row", "col"), None), P(("col", "row"), None), P()),
        out_specs=(P(("row", "col"), None), P(("col", "row"), None), P()),
        check_vma=False,
    )
```

time: 471 us -> 114 us (0.24)
  blocking collectives: 231 us -> 0 us
  waiting for transfers between devices: 122 us -> 0 us
  Pallas kernels: 0 us -> 108 us
  other arithmetic: 54.1 us -> 0 us
  matrix products: 43 us -> 0 us
  between operations: 14.5 us -> 3.06 us
    psum x3 -> x0, blocking collectives: 146 us -> none  [the longest x1 69.5 us: on_device(): lax.psum(jnp.sum(jnp.exp(logits - row_max[:, None]), axis=1), 'col')]
    pallas_call x0 -> x1, Pallas kernels: none -> 108 us  [on_device(): pl.pallas_call(kernel, out_shape=(jax.ShapeDtypeStruct((B, E), f32), jax....]
    pmax x2 -> x0, blocking collectives: 85 us -> none  [the longest x1 72.4 us: on_device(): row_max = lax.pmax(jnp.max(logits, axis=1), 'col')]
    all_gather x2 -> x0, waiting for transfers between devices: 81.1 us -> none  [the longest x1 54.5 us: on_device(): images = lax.all_gather(image_half, 'col', axis=0, tiled=True)]
    reduce_sum x3 -> x0, other arithmetic: 50.6 us -> none  [the longest x1 22 us: on_device(): partial_scale = jnp.sum(logit_grad * similar)]
    dot_general x3 -> x0, matrix products: 43 us -> none  [the longest x1 17.8 us: on_device(): lax.dot_general(images, text_cols, (((1,), (1,)), ((), ())), preferred_el...]
    reduce_scatter x2 -> x0, waiting for transfers between devices: 41.2 us -> none  [the longest x1 41.2 us: on_device(): lax.psum_scatter(logit_scale * jnp.dot(picked, text_cols, preferred_eleme...]
  transfers between devices with their start and end apart: 4 -> 0, of which waited for: 3 -> 0; matrix products, arithmetic and copies ran while one was open for 4% -> 0% of each run, Pallas kernels for 0% -> 0%
where the time goes in v1:
time: 114 us
  Pallas kernels  108 us (95%)
  between operations  3.06 us (3%)
  local copies, waits for them, and re-layouts  2.72 us (2%)
    pallas_call x1, Pallas kernels, on_device(): pl.pallas_call(kernel, out_shape=(jax.ShapeDtypeStruct((B, E), f32), jax....  108 us
    unnamed x4, local copies, waits for them, and re-layouts  2.72 us

profile of v1, /device:TPU:0, one launch (start us, length us, event | category | flops | bytes accessed | tf_op | source)
XLA Modules:
  0.0 114.1 jit_solution(7371281804385043379)
XLA Ops:
  1.3 108.3 %shard_map.58 = (f32[256,512]{1,0:T(8,128)}, f32[256,512]{1,0:T(8,128)}, f32[1,1]{1,0:T(1,128)}) custom-call(f32[1]{0:T(128)} %bitcast.2.scale_ref, f32[256,512]{1,0:T(8,128)} %img_hbm.1, f32[256,512]{1,0:T(8,128)} %txt_hbm.1), custom_call_target="tpu_custom_call" | custom-call | flops 25769803776 | bytes 4194304 | tf_op jit(solution)/shard_map/pallas_call | solution.py:585
  109.6 0.0 copy-start
  109.6 1.9 %copy.10 = f32[256,512]{1,0:T(8,128)} copy(f32[256,512]{1,0:T(8,128)} %get-tuple-element.12) | data formatting | bytes 1048576
  111.5 0.0 copy-done
  111.5 0.8 copy.11
Async XLA Ops:
  109.6 1.9 %copy-start = (f32[256,512]{1,0:T(8,128)S(1)}, f32[256,512]{1,0:T(8,128)}, u32[]{:S(2)}) copy-start(f32[256,512]{1,0:T(8,128)} %get-tuple-element.13) | copy-start | bytes 1572868

commit v2 on v1

--- a/solution.py
+++ b/solution.py
@@ -14,14 +14,20 @@
 B = 256
 E = 512
 H = B // 2
-KEPT = 6
+W = E // 2
+KEPT = 7
 
 IMG = ((0, 0), (0, 1), (1, 0), (3, 0), (2, 0), (1, 1), (3, 1), (2, 1))
 TXT = ((0, 0), (0, 1), (1, 0), (3, 0), (1, 1), (3, 1), (2, 0), (2, 1))
 TEXT_ORDER = (7, 5, 4, 6, 3, 2, 1, 0)
-
-GI, GT, SIB, RI, RT, DD = 0, 14, 28, 36, 49, 62
-ROWS, COLS, SC1, SC2, CHANNELS = 70, 86, 94, 110, 118
+UNITS = (
+    (0, 0, 2, 2, 0, 2, 5, 5, 5, 4, 4, 4, 0, 2, 5, 4),
+    (1, 1, 3, 3, 1, 3, 6, 6, 6, 7, 7, 7, 1, 3, 6, 7),
+    (0, 1, 0, 1, 2, 2, 0, 1, 2, 0, 1, 2, 3, 3, 3, 3),
+)
+
+GI, GT, SIB, RI, RT, DD = 0, 14, 28, 36, 50, 64
+ROWS, COLS, SC1, SC2, CHANNELS = 72, 88, 96, 112, 120
 
 
 def look_up(i, values):
@@ -46,7 +52,7 @@
 
 def kernel(
     scale_ref, img_hbm, txt_hbm, gi_hbm, gt_hbm, gs_ref,
-    I, T, LE, LO, TME, TMO, CME, CMO, GE, GO, MS, PB, XS, FR, XR, AR, FRT, XRT, ART,
+    I, T, LE, LO, TME, TMO, CME, CMO, GE, GO, MS, PB, XS, TS, PS, PST, FR, XR, AR, ARH, FRT, XRT, ART, ARHT,
     MC, SC, RSEND, RRECV, CSEND, CRECV, RLSE, CLSE, ACC, SR1, SR2,
     SS, RS, LS,
 ):
@@ -89,11 +95,6 @@
     I[0:B, :] = LE[0:B, 0:E].astype(bf16)
     load_t.wait()
     T[0:B, :] = LO[0:B, 0:E].astype(bf16)
-    MC[...] = jnp.full(MC.shape, -1e30, f32)
-    SC[...] = jnp.zeros(SC.shape, f32)
-    MS[:, :, 0:B] = jnp.full((8, B, B), -1e30, f32)
-    MS[:, :, B : 2 * B] = jnp.zeros((8, B, B), f32)
-    ACC[...] = jnp.zeros(ACC.shape, f32)
     pl.semaphore_wait(barrier, len(near))
 
     def gather(base, buf, step, slots, plus, minus, partner):
@@ -105,8 +106,10 @@
             ("own", (0, 0), partner, (0, 1), (0, 1)),
             ("own", (0, 0), plus, (3, 0), (0, 1)),
             ("own", (0, 0), minus, (1, 0), (1, 0)),
-            ("pair", (0, 1), plus, (3, 1), (0, 1)),
-            ("pair", (0, 1), minus, (1, 1), (1, 0)),
+            ("pair", (0, 1), plus, (3, 1), (0,)),
+            ("pair", (0, 1), minus, (1, 1), (1,)),
+            ("over", (3, 0), partner, (3, 1), (1,)),
+            ("over", (1, 0), partner, (1, 1), (0,)),
             ("on", (3, 0), plus, (2, 0), (0,)),
             ("on", (1, 0), minus, (2, 0), (1,)),
             ("on", (3, 1), plus, (2, 1), (0,)),
@@ -140,20 +143,29 @@
             gi[dst, h, (0, 0)].start()
             gt[dst, h, (0, 0)].start()
     sb[0, 0].start()
+    MC[...] = jnp.full(MC.shape, -1e30, f32)
+    SC[...] = jnp.zeros(SC.shape, f32)
+    MS[:, :, 0:B] = jnp.full((8, B, B), -1e30, f32)
+    MS[:, :, B : 2 * B] = jnp.zeros((8, B, B), f32)
+    ACC[...] = jnp.zeros(ACC.shape, f32)
+
+    def images(i):
+        return I[pl.ds(pl.multiple_of(i * 2 * B, 2 * B), 2 * B), :]
 
     def logit_tile(i, jp, e):
-        xt = lax.dot_general(
-            I[pl.ds(pl.multiple_of(i * 2 * B, 2 * B), 2 * B), :],
-            T[pl.ds(pl.multiple_of(jp * 2 * B + e * B, B), B), :],
-            NT, preferred_element_type=f32,
-        )
-        return xt * c2
+        rows = pl.ds(pl.multiple_of(jp * 2 * B + e * B, B), B)
+        return c2 * lax.dot_general(images(i), T[rows, :], NT, preferred_element_type=f32)
+
+    def turn(*slots):
+        for s in slots:
+            GE[0:E, s * B : (s + 1) * B] = T[s * B : (s + 1) * B, :].T
 
     def lrow(i):
         return pl.multiple_of(jnp.minimum(i, KEPT - 1) * 2 * B, 2 * B)
 
     def mm_section(i, jp, e):
-        xt = logit_tile(i, jp, e)
+        cols = pl.ds(pl.multiple_of(jp * 2 * B + e * B, B), B)
+        xt = c2 * jnp.dot(images(i), GE[0:E, cols], preferred_element_type=f32)
         L[e][pl.ds(lrow(i), 2 * B), pl.ds(pl.multiple_of(jp * B, B), B)] = xt
         TM[e][...] = jnp.maximum(xt[:, :128], xt[:, 128:])
         CM[e][...] = jnp.max(xt.reshape(2 * B // 8, 8, B), axis=0)
@@ -178,79 +190,77 @@
                 acc = acc + jnp.sum(jnp.exp2(l.reshape(U // 8, 8, B) - mc[None]), axis=0)
         SC[:, cols] = acc
 
-    def body(i, jp, prev):
-        st_section(prev[0], prev[1], 1)
-        mm_section(i, jp, 0)
-        st_section(i, jp, 0)
-        mm_section(i, jp, 1)
-        return (i, jp)
-
-    def sweep(n, index, prev):
-        def one(t, carry):
-            i, jp = index(t)
-            return body(i, jp, carry)
-
-        return lax.fori_loop(0, n, one, prev)
-
     for cps in (gi, gt):
         come(cps, (0, 1), 0)
         cps[(3, 1), 0, (0, 1)].start()
-    for cps in (gi, gt):
-        come(cps, (0, 1), 1)
-        cps[(1, 1), 1, (0, 1)].start()
-        cps[(3, 1), 1, (0, 1)].start()
-        cps[(1, 1), 0, (0, 1)].start()
-    for cps in (gi, gt):
         come(cps, (3, 0), 0)
         cps[(2, 0), 0, (3, 0)].start()
         come(cps, (1, 0), 1)
         cps[(2, 0), 1, (1, 0)].start()
+    for cps in (gi, gt):
+        come(cps, (0, 1), 1)
+        cps[(1, 1), 1, (0, 1)].start()
+        come(cps, (3, 0), 1)
+        cps[(3, 1), 1, (3, 0)].start()
+        come(cps, (1, 0), 0)
+        cps[(1, 1), 0, (1, 0)].start()
     sb[0, 1].start()
-    for cps in (gi, gt):
-        come(cps, (3, 0), 1)
-        come(cps, (1, 0), 0)
     sb[3, 0].start()
     sb[1, 0].start()
     for p in ((0, 0), (0, 1), (3, 0), (1, 0)):
         sb[p].wait_recv()
 
     zero = jnp.int32(0)
+
+    def second():
+        for cps in (gi, gt):
+            come(cps, (3, 1), 0)
+            cps[(2, 1), 0, (3, 1)].start()
+            come(cps, (1, 1), 1)
+            cps[(2, 1), 1, (1, 1)].start()
+        for cps in (gi, gt):
+            come(cps, (3, 1), 1)
+            come(cps, (1, 1), 0)
+        sb[3, 1].start()
+        sb[1, 1].start()
+        turn(4, 5)
+
+    def fifth():
+        sb[3, 1].wait_recv()
+        sb[1, 1].wait_recv()
+
+    def eighth():
+        for p in ((2, 0), (2, 1)):
+            for h in (0, 1):
+                come(gi, p, h)
+            sb[p].start()
+        sb[2, 0].wait_recv()
+        sb[2, 1].wait_recv()
+
+    def eleventh():
+        for p in ((2, 0), (2, 1)):
+            for h in (0, 1):
+                come(gt, p, h)
+        turn(6, 7)
+
+    def unit(t, carry):
+        for n, f in ((3, second), (5, fifth), (8, eighth), (11, eleventh)):
+            pl.when(t == n)(f)
+        i1, i2, jp = (look_up(t, v) for v in UNITS)
+        n1, _, njp = (look_up(t + 1, v) for v in UNITS)
+        st_section(i1, jp, 0)
+        mm_section(i1, jp, 1)
+        st_section(i1, jp, 1)
+        mm_section(i2, jp, 0)
+        st_section(i2, jp, 0)
+        mm_section(i2, jp, 1)
+        st_section(i2, jp, 1)
+        mm_section(n1, njp, 0)
+        return carry
+
+    turn(0, 1, 2, 3)
     mm_section(zero, zero, 0)
-    st_section(zero, zero, 0)
-    mm_section(zero, zero, 1)
-    prev = (zero, zero)
-    prev = sweep(7, lambda t: ((t + 1) // 2, (t + 1) % 2), prev)
-
-    for cps in (gi, gt):
-        come(cps, (3, 1), 0)
-        cps[(2, 1), 0, (3, 1)].start()
-        come(cps, (1, 1), 1)
-        cps[(2, 1), 1, (1, 1)].start()
-    for cps in (gi, gt):
-        come(cps, (3, 1), 1)
-        come(cps, (1, 1), 0)
-    sb[3, 1].start()
-    sb[1, 1].start()
-    prev = sweep(4, lambda t: (t, zero + 2), prev)
-    sb[3, 1].wait_recv()
-    sb[1, 1].wait_recv()
-    prev = sweep(6, lambda t: (5 + t // 3, t % 3), prev)
-
-    come(gi, (2, 0), 0)
-    come(gi, (2, 0), 1)
-    sb[2, 0].start()
-    sb[2, 0].wait_recv()
-    prev = sweep(3, lambda t: (zero + 4, t), prev)
-    for p in ((2, 0), (2, 1)):
-        for h in (0, 1):
-            come(gt, p, h)
-    come(gi, (2, 1), 0)
-    come(gi, (2, 1), 1)
-    sb[2, 1].start()
-    prev = sweep(7, lambda t: (t, zero + 3), prev)
-    sb[2, 1].wait_recv()
-    prev = sweep(4, lambda t: (zero + 7, t), prev)
-    st_section(prev[0], prev[1], 1)
+    lax.fori_loop(0, 16, unit, 0)
 
     eye = lax.broadcasted_iota(jnp.int32, (128, 128), 0) == lax.broadcasted_iota(jnp.int32, (128, 128), 1)
 
@@ -308,10 +318,12 @@
     for cp in [*gi.values(), *gt.values(), *sb.values()]:
         cp.wait_send()
 
-    def row_col(i, q, h):
-        v = RLSE[pl.ds(image_block(i, q) * 2 + h, 1), :]
-        v = jnp.sum(jnp.where(eye, jnp.broadcast_to(v, (128, 128)), 0.0), axis=1, keepdims=True)
-        return jnp.broadcast_to(v, (128, 128))
+    def spread_rows(i, e):
+        for q in (0, 1):
+            for h in (0, 1):
+                v = RLSE[pl.ds(image_block(i, q) * 2 + h, 1), :]
+                v = jnp.sum(jnp.where(eye, jnp.broadcast_to(v, (128, 128)), 0.0), axis=1, keepdims=True)
+                TM[e][q * B + h * 128 : q * B + (h + 1) * 128] = jnp.broadcast_to(v, (128, 128))
 
     def grow(i):
         return pl.multiple_of((i // 2) * 2 * B, 2 * B)
@@ -321,7 +333,7 @@
         acc = ACC[...]
         for q in (0, 1):
             for h in (0, 1):
-                rl = row_col(i, q, h)
+                rl = TM[e][q * B + h * 128 : q * B + (h + 1) * 128]
                 for u in range(128 // U):
                     off = q * B + h * 128 + u * U
                     rb = rl[u * U : (u + 1) * U]
@@ -349,7 +361,7 @@
                         rows = q * B + h * 128
                         l = L[e][pl.ds(lrow(i) + rows, 128), pl.ds(pl.multiple_of((j // 2) * B + h * 128, 128), 128)]
                         cl = MC[0:1, pl.ds(pl.multiple_of(j * B + h * 128, 128), 128)]
-                        g = jnp.exp2(l - row_col(i, q, h)) + jnp.exp2(l - cl)
+                        g = jnp.exp2(l - TM[par][rows : rows + 128]) + jnp.exp2(l - cl)
                         g = jnp.where(eye, g - 1.0, g)
                         G[par][
                             pl.ds(grow(i) + rows, 128),
@@ -363,7 +375,7 @@
         PB[e, 0] = p[:B]
         PB[e, 1] = p[B:]
 
-    def scatter(base, src, own, fr, xr, ar, plus, minus, partner):
+    def scatter(base, src, own, own_half, fr, xr, ar, ar_half, plus, minus, partner):
         out = {}
         for n, p in enumerate((1, 0)):
             s, lo, hi = base + 6 * n, slice(0, H), slice(H, B)
@@ -373,15 +385,16 @@
             out[1, p, 1] = chan(s + 3, src((1, p)).at[hi], xr.at[0, p, hi], plus)
             out[3, p, 0] = chan(s + 4, src((3, p)).at[lo], xr.at[1, p, lo], minus)
             out[3, p, 1] = chan(s + 5, src((3, p)).at[hi], xr.at[1, p, hi], minus)
-        out[0, 1] = chan(base + 12, own, ar, partner)
+        out[0, 1, 0] = chan(base + 12, own.at[:, 0:W], ar, partner)
+        out[0, 1, 1] = chan(base + 13, own_half, ar_half, partner)
         return out
 
-    stage = {(2, 1): 0, (3, 1): 1, (1, 1): 2, (2, 0): 3, (3, 0): 0, (1, 0): 1}
+    stage = {(2, 1): 0, (3, 1): 1, (1, 1): 2, (2, 0): 0, (3, 0): 1, (1, 0): 2}
     xs = lambda place: XS.at[stage[place]]
-    ts = lambda place: T.at[TXT.index(place) * B : (TXT.index(place) + 1) * B]
+    ts = lambda place: TS.at[stage[place]]
     ltext = lambda s: LE.at[s * B : (s + 1) * B, 0:E]
-    ri = scatter(RI, xs, MS.at[1], FR, XR, AR, xp, xm, pa)
-    rt = scatter(RT, ts, ltext(1), FRT, XRT, ART, zp, zm, pb)
+    ri = scatter(RI, xs, MS.at[1], PS, FR, XR, AR, ARH, xp, xm, pa)
+    rt = scatter(RT, ts, ltext(1), PST, FRT, XRT, ART, ARHT, zp, zm, pb)
 
     def across(i, e):
         return chan(DD + i, PB.at[e, 1], MS.at[i], sib)
@@ -389,7 +402,13 @@
     def half(h):
         return pl.ds(h * H, H)
 
+    def free(cps, place):
+        if place[1] == 0:
+            for h in (0, 1):
+                cps[place[0], 1, h].wait_send()
+
     def send_far(cps, place, p, stage_ref):
+        free(cps, place)
         stage_ref[...] = p[...].astype(bf16)
         cps[(*place, 0)].start()
         cps[(*place, 1)].start()
@@ -398,6 +417,7 @@
 
     def send_pure(cps, place, p, stage_ref):
         h = 1 - mixed[place[0]]
+        free(cps, place)
         stage_ref[half(h)] = p[half(h)].astype(bf16)
         cps[(*place, h)].start()
 
@@ -412,24 +432,20 @@
             for h in (0, 1):
                 cps[ring, pair, h].wait_recv()
 
-    def send_pair(cps, p, xr):
+    def send_pair(cps, p, half_ref, xr):
         arrived(cps, 1)
         p[...] += xr[0, 1].astype(f32) + xr[1, 1].astype(f32)
-        cps[0, 1].start()
-
-    frees = {(3, 0): (2, 1), (1, 0): (3, 1)}
-    waited = [(*frees[p], h) for p in frees for h in (0, 1)]
+        half_ref[...] = p[:, W:E].astype(bf16)
+        cps[0, 1, 0].start()
+        cps[0, 1, 1].start()
 
     def image_sum(s):
         place = IMG[s]
         across(s, s % 2).wait_recv()
         MS[s] += PB[s % 2, 0]
-        if place in frees:
-            for h in (0, 1):
-                ri[(*frees[place], h)].wait_send()
         if place[0] == 2:
             send_far(ri, place, MS.at[s], xs(place))
-        elif place[0]:
+        elif place[0] % 2:
             send_pure(ri, place, MS.at[s], xs(place))
         across(s, s % 2).wait_send()
 
@@ -447,6 +463,7 @@
         again(i)
         grads(i, e)
         image_product(i + 1, 1 - e)
+        spread_rows(jnp.maximum(i - 1, 0), 1 - e)
         matched(i, e)
         across(i + 1, 1 - e).start()
         for s in range(7, 1, -1):
@@ -468,7 +485,9 @@
         return carry
 
     seven = jnp.int32(7)
+    spread_rows(seven, 1)
     grads(seven, 1)
+    spread_rows(seven - 1, 0)
     matched(seven, 1)
     lax.fori_loop(0, 3, g_step, 0)
     g_half(zero, 0)
@@ -480,9 +499,6 @@
         here = dk * 8 + da * 4 + (4 - dx) % 4
         sc1_out.append(chan(SC1 + here, ACC, SR1.at[mine], dev(dx=dx, da=da, dk=dk)))
         sc1_out[-1].start()
-
-    image_product(zero, 0)
-    across(zero, 0).start()
 
     mine_t = text_block(zero)
     sc2_out = [
@@ -508,29 +524,30 @@
         @pl.when(t == 0)
         def _():
             text_send(send_far, (2, 1))
+
+        @pl.when(t == 1)
+        def _():
+            text_send(send_pure, (3, 1))
             image_sum(1)
-            image_sum(0)
+
+        @pl.when(t == 2)
+        def _():
+            text_send(send_pure, (1, 1))
             image_mixed((3, 0))
             image_mixed((1, 0))
-
-        @pl.when(t == 1)
-        def _():
-            text_send(send_pure, (3, 1))
-
-        @pl.when(t == 2)
-        def _():
-            text_send(send_pure, (1, 1))
 
         @pl.when(t == 3)
         def _():
             text_send(send_mixed, (3, 1), FRT)
             text_send(send_mixed, (1, 1), FRT)
             text_send(send_far, (2, 0))
+            send_pair(ri, MS.at[1], PS, XR)
 
         @pl.when(t == 4)
         def _():
             text_send(send_pure, (3, 0))
-            send_pair(ri, MS.at[1], XR)
+            image_product(zero, 0)
+            across(zero, 0).start()
 
         @pl.when(t == 5)
         def _():
@@ -542,8 +559,13 @@
             for cp in sc2_out:
                 cp.start()
 
+        @pl.when(t == 6)
+        def _():
+            image_sum(0)
+
         @pl.when(t == 7)
         def _():
+            send_pair(rt, ltext(1), PST, XRT)
             text_send(send_mixed, (3, 0), FRT)
             text_send(send_mixed, (1, 0), FRT)
 
@@ -551,29 +573,29 @@
 
     lax.fori_loop(0, 8, text_step, 0)
 
-    def finish(cps, p, xr, ar, out, sem):
+    def finish(cps, p, xr, ar, ar_half, out, sem):
         arrived(cps, 0)
         p[...] += xr[0, 0].astype(f32) + xr[1, 0].astype(f32)
-        cps[0, 1].wait_recv()
-        p[...] = scale * (p[...] + ar[...])
+        cps[0, 1, 0].wait_recv()
+        cps[0, 1, 1].wait_recv()
+        p[:, 0:W] = scale * (p[:, 0:W] + ar[...])
+        p[:, W:E] = scale * (p[:, W:E] + ar_half[...].astype(f32))
         store = pltpu.make_async_copy(p, out, sem)
         store.start()
         return store
 
-    send_pair(rt, ltext(1), XRT)
     for cp in sc2_out:
         cp.wait()
     gs_ref[0, 0] = jnp.sum(sum(SR2[n] for n in range(8))) / c2
-    store_i = finish(ri, MS.at[0], XR, AR, gi_hbm, LS.at[0])
-    store_t = finish(rt, ltext(0), XRT, ART, gt_hbm, LS.at[1])
+    store_i = finish(ri, MS.at[0], XR, AR, ARH, gi_hbm, LS.at[0])
+    store_t = finish(rt, ltext(0), XRT, ART, ARHT, gt_hbm, LS.at[1])
 
     for cp in rows_out + cols_out:
         cp.wait_send()
-    for name, cp in ri.items():
-        if name not in waited:
-            cp.wait_send()
-    for cp in rt.values():
-        cp.wait_send()
+    for cps in (ri, rt):
+        for (ring, pair, _), cp in cps.items():
+            if ring == 0 or pair == 0:
+                cp.wait_send()
     store_i.wait()
     store_t.wait()
 
@@ -604,13 +626,18 @@
             pltpu.VMEM((8 * B, 8 * B), bf16),
             pltpu.VMEM((8, B, E), f32),
             pltpu.VMEM((2, 2, B, E), f32),
-            pltpu.VMEM((4, B, E), bf16),
+            pltpu.VMEM((3, B, E), bf16),
+            pltpu.VMEM((3, B, E), bf16),
+            pltpu.VMEM((B, E - W), bf16),
+            pltpu.VMEM((B, E - W), bf16),
             pltpu.VMEM((2, 2, H, E), bf16),
             pltpu.VMEM((2, 2, B, E), bf16),
-            pltpu.VMEM((B, E), f32),
+            pltpu.VMEM((B, W), f32),
+            pltpu.VMEM((B, E - W), bf16),
             pltpu.VMEM((2, 2, H, E), bf16),
             pltpu.VMEM((2, 2, B, E), bf16),
-            pltpu.VMEM((B, E), f32),
+            pltpu.VMEM((B, W), f32),
+            pltpu.VMEM((B, E - W), bf16),
             pltpu.VMEM((8, 8 * B), f32),
             pltpu.VMEM((8, 8 * B), f32),
             pltpu.VMEM((32, 128), f32),

time: 114 us -> 104 us (0.912)
  Pallas kernels: 108 us -> 98.4 us
    pallas_call x1, Pallas kernels: 108 us -> 98.4 us  [on_device(): pl.pallas_call(kernel, out_shape=(jax.ShapeDtypeStruct((B, E), f32), jax....]
where the time goes in v2:
time: 104 us
  Pallas kernels  98.4 us (95%)
  between operations  3.06 us (3%)
  local copies, waits for them, and re-layouts  2.72 us (3%)
    pallas_call x1, Pallas kernels, on_device(): pl.pallas_call(kernel, out_shape=(jax.ShapeDtypeStruct((B, E), f32), jax....  98.4 us
    unnamed x4, local copies, waits for them, and re-layouts  2.72 us

profile of v2, /device:TPU:0, one launch (start us, length us, event | category | flops | bytes accessed | tf_op | source)
XLA Modules:
  0.0 104.2 jit_solution(9297735207415625295)
XLA Ops:
  1.3 98.4 %shard_map.58 = (f32[256,512]{1,0:T(8,128)}, f32[256,512]{1,0:T(8,128)}, f32[1,1]{1,0:T(1,128)}) custom-call(f32[1]{0:T(128)} %bitcast.2.scale_ref, f32[256,512]{1,0:T(8,128)} %img_hbm.1, f32[256,512]{1,0:T(8,128)} %txt_hbm.1), custom_call_target="tpu_custom_call" | custom-call | flops 25769803776 | bytes 4194304 | tf_op jit(solution)/shard_map/pallas_call | solution.py:607
  99.7 0.0 copy-start
  99.7 1.9 %copy.10 = f32[256,512]{1,0:T(8,128)} copy(f32[256,512]{1,0:T(8,128)} %get-tuple-element.12) | data formatting | bytes 1048576
  101.6 0.0 copy-done
  101.6 0.8 copy.11
Async XLA Ops:
  99.7 1.9 %copy-start = (f32[256,512]{1,0:T(8,128)S(1)}, f32[256,512]{1,0:T(8,128)}, u32[]{:S(2)}) copy-start(f32[256,512]{1,0:T(8,128)} %get-tuple-element.13) | copy-start | bytes 1572868

commit v3 on v2

--- a/solution.py
+++ b/solution.py
@@ -15,16 +15,12 @@
 E = 512
 H = B // 2
 W = E // 2
-KEPT = 7
+KEPT = 2
 
 IMG = ((0, 0), (0, 1), (1, 0), (3, 0), (2, 0), (1, 1), (3, 1), (2, 1))
 TXT = ((0, 0), (0, 1), (1, 0), (3, 0), (1, 1), (3, 1), (2, 0), (2, 1))
 TEXT_ORDER = (7, 5, 4, 6, 3, 2, 1, 0)
-UNITS = (
-    (0, 0, 2, 2, 0, 2, 5, 5, 5, 4, 4, 4, 0, 2, 5, 4),
-    (1, 1, 3, 3, 1, 3, 6, 6, 6, 7, 7, 7, 1, 3, 6, 7),
-    (0, 1, 0, 1, 2, 2, 0, 1, 2, 0, 1, 2, 3, 3, 3, 3),
-)
+EVEN, ODD = (0, 2, 6, 4), (1, 3, 5, 7)
 
 GI, GT, SIB, RI, RT, DD = 0, 14, 28, 36, 50, 64
 ROWS, COLS, SC1, SC2, CHANNELS = 72, 88, 96, 112, 120
@@ -152,26 +148,26 @@
     def images(i):
         return I[pl.ds(pl.multiple_of(i * 2 * B, 2 * B), 2 * B), :]
 
-    def logit_tile(i, jp, e):
-        rows = pl.ds(pl.multiple_of(jp * 2 * B + e * B, B), B)
-        return c2 * lax.dot_general(images(i), T[rows, :], NT, preferred_element_type=f32)
-
-    def turn(*slots):
-        for s in slots:
-            GE[0:E, s * B : (s + 1) * B] = T[s * B : (s + 1) * B, :].T
-
-    def lrow(i):
-        return pl.multiple_of(jnp.minimum(i, KEPT - 1) * 2 * B, 2 * B)
+    def images(i):
+        return I[pl.ds(pl.multiple_of(i * 2 * B, 2 * B), 2 * B), :]
+
+    def logit_tile(i, j):
+        return c2 * lax.dot_general(images(i), T[j * B : (j + 1) * B, :], NT, preferred_element_type=f32)
+
+    def lrow(i, e):
+        return pl.multiple_of((jnp.minimum(i // 2, KEPT - 1) if e else i // 2) * 2 * B, 2 * B)
 
     def mm_section(i, jp, e):
-        cols = pl.ds(pl.multiple_of(jp * 2 * B + e * B, B), B)
-        xt = c2 * jnp.dot(images(i), GE[0:E, cols], preferred_element_type=f32)
-        L[e][pl.ds(lrow(i), 2 * B), pl.ds(pl.multiple_of(jp * B, B), B)] = xt
-        TM[e][...] = jnp.maximum(xt[:, :128], xt[:, 128:])
-        CM[e][...] = jnp.max(xt.reshape(2 * B // 8, 8, B), axis=0)
+        for n in (0, 1):
+            j = 2 * jp + n
+            xt = logit_tile(i, j)
+            L[e][pl.ds(lrow(i, e), 2 * B), j * B : (j + 1) * B] = xt
+            top = jnp.maximum(xt[:, :128], xt[:, 128:])
+            TM[e][...] = jnp.maximum(TM[e][...], top) if n else top
+            CM[e][:, n * B : (n + 1) * B] = jnp.max(xt.reshape(2 * B // 8, 8, B), axis=0)
 
     def st_section(i, jp, e):
-        cols = pl.ds(pl.multiple_of(jp * 2 * B + e * B, B), B)
+        cols = slice(jp * 2 * B, (jp + 1) * 2 * B)
         old = MC[:, cols]
         mc = jnp.maximum(old, CM[e][...])
         MC[:, cols] = mc
@@ -179,15 +175,16 @@
         U = 64
         for q in (0, 1):
             for u in range(B // U):
-                l = L[e][pl.ds(lrow(i) + q * B + u * U, U), pl.ds(pl.multiple_of(jp * B, B), B)]
+                l = L[e][pl.ds(lrow(i, e) + q * B + u * U, U), cols]
                 rows, mcol, scol = slice(u * U, (u + 1) * U), slice(q * 128, (q + 1) * 128), slice(B + q * 128, B + (q + 1) * 128)
                 old = MS[i, rows, mcol]
                 m = jnp.maximum(old, TM[e][q * B + u * U : q * B + (u + 1) * U])
                 MS[i, rows, mcol] = m
-                MS[i, rows, scol] = (
-                    MS[i, rows, scol] * jnp.exp2(old - m) + jnp.exp2(l[:, :128] - m) + jnp.exp2(l[:, 128:] - m)
-                )
-                acc = acc + jnp.sum(jnp.exp2(l.reshape(U // 8, 8, B) - mc[None]), axis=0)
+                s = MS[i, rows, scol] * jnp.exp2(old - m)
+                for v in range(4):
+                    s = s + jnp.exp2(l[:, v * 128 : (v + 1) * 128] - m)
+                MS[i, rows, scol] = s
+                acc = acc + jnp.sum(jnp.exp2(l.reshape(U // 8, 8, 2 * B) - mc[None]), axis=0)
         SC[:, cols] = acc
 
     for cps in (gi, gt):
@@ -223,13 +220,8 @@
             come(cps, (1, 1), 0)
         sb[3, 1].start()
         sb[1, 1].start()
-        turn(4, 5)
-
-    def fifth():
-        sb[3, 1].wait_recv()
-        sb[1, 1].wait_recv()
-
-    def eighth():
+
+    def third():
         for p in ((2, 0), (2, 1)):
             for h in (0, 1):
                 come(gi, p, h)
@@ -237,30 +229,39 @@
         sb[2, 0].wait_recv()
         sb[2, 1].wait_recv()
 
-    def eleventh():
-        for p in ((2, 0), (2, 1)):
-            for h in (0, 1):
-                come(gt, p, h)
-        turn(6, 7)
-
-    def unit(t, carry):
-        for n, f in ((3, second), (5, fifth), (8, eighth), (11, eleventh)):
-            pl.when(t == n)(f)
-        i1, i2, jp = (look_up(t, v) for v in UNITS)
-        n1, _, njp = (look_up(t + 1, v) for v in UNITS)
-        st_section(i1, jp, 0)
-        mm_section(i1, jp, 1)
-        st_section(i1, jp, 1)
-        mm_section(i2, jp, 0)
-        st_section(i2, jp, 0)
-        mm_section(i2, jp, 1)
-        st_section(i2, jp, 1)
-        mm_section(n1, njp, 0)
-        return carry
-
-    turn(0, 1, 2, 3)
-    mm_section(zero, zero, 0)
-    lax.fori_loop(0, 16, unit, 0)
+    def pairs(first, count, jps, ahead, before=None):
+        last = first + count - 1
+
+        def one(t, carry):
+            if before is not None:
+                pl.when(t == last)(before)
+            ev, od = look_up(t, EVEN), look_up(t, ODD)
+            if not ahead:
+                mm_section(ev, jps[0], 0)
+            for n, jp in enumerate(jps):
+                st_section(ev, jp, 0)
+                mm_section(od, jp, 1)
+                st_section(od, jp, 1)
+                if n + 1 < len(jps):
+                    mm_section(ev, jps[n + 1], 0)
+                elif ahead:
+                    mm_section(look_up(jnp.minimum(t + 1, last), EVEN), jps[0], 0)
+            return carry
+
+        if ahead:
+            mm_section(jnp.int32(EVEN[first]), jps[0], 0)
+        lax.fori_loop(first, first + count, one, 0)
+
+    pairs(0, 2, (0, 1), True)
+    second()
+    pairs(0, 2, (2,), True)
+    sb[3, 1].wait_recv()
+    sb[1, 1].wait_recv()
+    pairs(2, 2, (0, 1, 2), False, third)
+    for p in ((2, 0), (2, 1)):
+        for h in (0, 1):
+            come(gt, p, h)
+    pairs(0, 4, (3,), True)
 
     eye = lax.broadcasted_iota(jnp.int32, (128, 128), 0) == lax.broadcasted_iota(jnp.int32, (128, 128), 1)
 
@@ -339,7 +340,7 @@
                     rb = rl[u * U : (u + 1) * U]
                     rb = jnp.concatenate([rb, rb], axis=1)
                     for j in range(8):
-                        l = L[j % 2][pl.ds(lrow(i) + off, U), (j // 2) * B : (j // 2 + 1) * B]
+                        l = L[e][pl.ds(lrow(i, e) + off, U), j * B : (j + 1) * B]
                         cl = MC[:, j * B : (j + 1) * B]
                         g = jnp.exp2(l - rb) + jnp.exp2(l.reshape(U // 8, 8, B) - cl[None]).reshape(U, B)
                         w = jnp.sum((g * l).reshape(U // 8, 8, B), axis=0)
@@ -353,22 +354,18 @@
         here = (x % 2 == b) & ((z + z // 2) % 2 == a) & (xi % 2 == k)
         j = text_slot((2 * (yi % 2) + xi // 2 - z + 4) % 4, (z // 2 + b) % 2)
         for q in (0, 1):
-            for e in (0, 1):
-
-                @pl.when(here & ((k + q) % 2 == x // 2) & (j % 2 == e))
-                def _():
-                    for h in (0, 1):
-                        rows = q * B + h * 128
-                        l = L[e][pl.ds(lrow(i) + rows, 128), pl.ds(pl.multiple_of((j // 2) * B + h * 128, 128), 128)]
-                        cl = MC[0:1, pl.ds(pl.multiple_of(j * B + h * 128, 128), 128)]
-                        g = jnp.exp2(l - TM[par][rows : rows + 128]) + jnp.exp2(l - cl)
-                        g = jnp.where(eye, g - 1.0, g)
-                        G[par][
-                            pl.ds(grow(i) + rows, 128),
-                            pl.ds(pl.multiple_of(j * B + h * 128, 128), 128),
-                        ] = g.astype(bf16)
-                        w = jnp.where(eye, l, 0.0)
-                        ACC[...] -= jnp.sum(w.reshape(16, 8, 128), axis=0)
+
+            @pl.when(here & ((k + q) % 2 == x // 2))
+            def _():
+                for h in (0, 1):
+                    rows = q * B + h * 128
+                    cols = pl.ds(pl.multiple_of(j * B + h * 128, 128), 128)
+                    l = L[par][pl.ds(lrow(i, par) + rows, 128), cols]
+                    g = jnp.exp2(l - TM[par][rows : rows + 128]) + jnp.exp2(l - MC[0:1, cols])
+                    g = jnp.where(eye, g - 1.0, g)
+                    G[par][pl.ds(grow(i) + rows, 128), cols] = g.astype(bf16)
+                    w = jnp.where(eye, l, 0.0)
+                    ACC[...] -= jnp.sum(w.reshape(16, 8, 128), axis=0)
 
     def image_product(i, e):
         p = jnp.dot(G[e][pl.ds(grow(i), 2 * B), :], T[...], preferred_element_type=f32)
@@ -453,14 +450,12 @@
         send_mixed(ri, place, MS.at[IMG.index(place)], xs(place), FR)
 
     def again(i):
-        @pl.when((i >= KEPT - 1) & (i < 7))
-        def _():
-            for e in (0, 1):
-                for jp in range(4):
-                    L[e][(KEPT - 1) * 2 * B : KEPT * 2 * B, jp * B : (jp + 1) * B] = logit_tile(i, jp, e)
+        for j in range(8):
+            L[1][(KEPT - 1) * 2 * B : KEPT * 2 * B, j * B : (j + 1) * B] = logit_tile(i, j)
 
     def g_half(i, e):
-        again(i)
+        if e:
+            pl.when(i >= 2 * KEPT - 1)(lambda: again(i))
         grads(i, e)
         image_product(i + 1, 1 - e)
         spread_rows(jnp.maximum(i - 1, 0), 1 - e)
@@ -616,12 +611,12 @@
         scratch_shapes=[
             pltpu.VMEM((16 * B, E), bf16),
             pltpu.VMEM((8 * B, E), bf16),
-            pltpu.VMEM((KEPT * 2 * B, 4 * B), f32),
-            pltpu.VMEM((KEPT * 2 * B, 4 * B), f32),
+            pltpu.VMEM((8 * B, 8 * B), f32),
+            pltpu.VMEM((KEPT * 2 * B, 8 * B), f32),
             pltpu.VMEM((2 * B, 128), f32),
             pltpu.VMEM((2 * B, 128), f32),
-            pltpu.VMEM((8, B), f32),
-            pltpu.VMEM((8, B), f32),
+            pltpu.VMEM((8, 2 * B), f32),
+            pltpu.VMEM((8, 2 * B), f32),
             pltpu.VMEM((8 * B, 8 * B), bf16),
             pltpu.VMEM((8 * B, 8 * B), bf16),
             pltpu.VMEM((8, B, E), f32),

time: 104 us -> 101 us (0.971)
  Pallas kernels: 98.4 us -> 94.6 us
    pallas_call x1, Pallas kernels: 98.4 us -> 94.6 us  [on_device(): pl.pallas_call(kernel, out_shape=(jax.ShapeDtypeStruct((B, E), f32), jax....]
where the time goes in v3:
time: 101 us; the launch traced here: 100 us
  Pallas kernels  94.6 us (94%)
  between operations  3.06 us (3%)
  local copies, waits for them, and re-layouts  2.72 us (3%)
    pallas_call x1, Pallas kernels, on_device(): pl.pallas_call(kernel, out_shape=(jax.ShapeDtypeStruct((B, E), f32), jax....  94.6 us
    unnamed x4, local copies, waits for them, and re-layouts  2.72 us

profile of v3, /device:TPU:0, one launch (start us, length us, event | category | flops | bytes accessed | tf_op | source)
XLA Modules:
  0.0 100.4 jit_solution(1904791957230548134)
XLA Ops:
  1.3 94.6 %shard_map.58 = (f32[256,512]{1,0:T(8,128)}, f32[256,512]{1,0:T(8,128)}, f32[1,1]{1,0:T(1,128)}) custom-call(f32[1]{0:T(128)} %bitcast.2.scale_ref, f32[256,512]{1,0:T(8,128)} %img_hbm.1, f32[256,512]{1,0:T(8,128)} %txt_hbm.1), custom_call_target="tpu_custom_call" | custom-call | flops 25769803776 | bytes 4194304 | tf_op jit(solution)/shard_map/pallas_call | solution.py:602
  95.9 0.0 copy-start
  95.9 1.9 %copy.10 = f32[256,512]{1,0:T(8,128)} copy(f32[256,512]{1,0:T(8,128)} %get-tuple-element.12) | data formatting | bytes 1048576
  97.8 0.0 copy-done
  97.8 0.8 copy.11
Async XLA Ops:
  95.9 1.9 %copy-start = (f32[256,512]{1,0:T(8,128)S(1)}, f32[256,512]{1,0:T(8,128)}, u32[]{:S(2)}) copy-start(f32[256,512]{1,0:T(8,128)} %get-tuple-element.13) | copy-start | bytes 1572868

commit v4 on v3

--- a/solution.py
+++ b/solution.py
@@ -47,7 +47,7 @@
 
 
 def kernel(
-    scale_ref, img_hbm, txt_hbm, gi_hbm, gt_hbm, gs_ref,
+    scale_ref, img_hbm, txt_hbm, out_hbm, gs_ref,
     I, T, LE, LO, TME, TMO, CME, CMO, GE, GO, MS, PB, XS, TS, PS, PST, FR, XR, AR, ARH, FRT, XRT, ART, ARHT,
     MC, SC, RSEND, RRECV, CSEND, CRECV, RLSE, CLSE, ACC, SR1, SR2,
     SS, RS, LS,
@@ -215,26 +215,25 @@
             cps[(2, 1), 0, (3, 1)].start()
             come(cps, (1, 1), 1)
             cps[(2, 1), 1, (1, 1)].start()
-        for cps in (gi, gt):
-            come(cps, (3, 1), 1)
-            come(cps, (1, 1), 0)
-        sb[3, 1].start()
-        sb[1, 1].start()
-
-    def third():
+
+    def last():
         for p in ((2, 0), (2, 1)):
             for h in (0, 1):
                 come(gi, p, h)
             sb[p].start()
+        for p in ((2, 0), (2, 1)):
+            for h in (0, 1):
+                come(gt, p, h)
+        pairs(0, 3, (3,), True)
         sb[2, 0].wait_recv()
         sb[2, 1].wait_recv()
 
     def pairs(first, count, jps, ahead, before=None):
-        last = first + count - 1
+        end = first + count - 1
 
         def one(t, carry):
             if before is not None:
-                pl.when(t == last)(before)
+                pl.when(t == end)(before)
             ev, od = look_up(t, EVEN), look_up(t, ODD)
             if not ahead:
                 mm_section(ev, jps[0], 0)
@@ -245,23 +244,24 @@
                 if n + 1 < len(jps):
                     mm_section(ev, jps[n + 1], 0)
                 elif ahead:
-                    mm_section(look_up(jnp.minimum(t + 1, last), EVEN), jps[0], 0)
+                    mm_section(look_up(jnp.minimum(t + 1, end), EVEN), jps[0], 0)
             return carry
 
         if ahead:
             mm_section(jnp.int32(EVEN[first]), jps[0], 0)
         lax.fori_loop(first, first + count, one, 0)
 
-    pairs(0, 2, (0, 1), True)
-    second()
+    pairs(0, 2, (0, 1), True, second)
+    for cps in (gi, gt):
+        come(cps, (3, 1), 1)
+        come(cps, (1, 1), 0)
+    sb[3, 1].start()
+    sb[1, 1].start()
     pairs(0, 2, (2,), True)
     sb[3, 1].wait_recv()
     sb[1, 1].wait_recv()
-    pairs(2, 2, (0, 1, 2), False, third)
-    for p in ((2, 0), (2, 1)):
-        for h in (0, 1):
-            come(gt, p, h)
-    pairs(0, 4, (3,), True)
+    pairs(2, 2, (0, 1, 2), False, last)
+    pairs(3, 1, (3,), False)
 
     eye = lax.broadcasted_iota(jnp.int32, (128, 128), 0) == lax.broadcasted_iota(jnp.int32, (128, 128), 1)
 
@@ -315,9 +315,6 @@
     parts = [RSEND[...]] + [RRECV[n] for n in range(1, 16)]
     m = functools.reduce(jnp.maximum, parts)
     RLSE[...] = m + 1.0 + jnp.log2(sum(jnp.exp2(v - m) for v in parts))
-
-    for cp in [*gi.values(), *gt.values(), *sb.values()]:
-        cp.wait_send()
 
     def spread_rows(i, e):
         for q in (0, 1):
@@ -493,7 +490,6 @@
     for dx, da, dk in row_peers:
         here = dk * 8 + da * 4 + (4 - dx) % 4
         sc1_out.append(chan(SC1 + here, ACC, SR1.at[mine], dev(dx=dx, da=da, dk=dk)))
-        sc1_out[-1].start()
 
     mine_t = text_block(zero)
     sc2_out = [
@@ -523,30 +519,44 @@
         @pl.when(t == 1)
         def _():
             text_send(send_pure, (3, 1))
-            image_sum(1)
 
         @pl.when(t == 2)
         def _():
             text_send(send_pure, (1, 1))
-            image_mixed((3, 0))
-            image_mixed((1, 0))
 
         @pl.when(t == 3)
         def _():
             text_send(send_mixed, (3, 1), FRT)
             text_send(send_mixed, (1, 1), FRT)
             text_send(send_far, (2, 0))
+            image_sum(1)
             send_pair(ri, MS.at[1], PS, XR)
+            image_mixed((3, 0))
+            image_mixed((1, 0))
 
         @pl.when(t == 4)
         def _():
             text_send(send_pure, (3, 0))
             image_product(zero, 0)
             across(zero, 0).start()
+            for cp in sc1_out:
+                cp.start()
 
         @pl.when(t == 5)
         def _():
             text_send(send_pure, (1, 0))
+
+        @pl.when(t == 6)
+        def _():
+            image_sum(0)
+            for cp in [*gi.values(), *gt.values(), *sb.values(), *rows_out, *cols_out]:
+                cp.wait_send()
+
+        @pl.when(t == 7)
+        def _():
+            send_pair(rt, ltext(1), PST, XRT)
+            text_send(send_mixed, (3, 0), FRT)
+            text_send(send_mixed, (1, 0), FRT)
             for cp in sc1_out:
                 cp.wait()
             ACC[...] = sum(SR1[n] for n in range(16))
@@ -554,16 +564,6 @@
             for cp in sc2_out:
                 cp.start()
 
-        @pl.when(t == 6)
-        def _():
-            image_sum(0)
-
-        @pl.when(t == 7)
-        def _():
-            send_pair(rt, ltext(1), PST, XRT)
-            text_send(send_mixed, (3, 0), FRT)
-            text_send(send_mixed, (1, 0), FRT)
-
         return carry
 
     lax.fori_loop(0, 8, text_step, 0)
@@ -573,8 +573,8 @@
         p[...] += xr[0, 0].astype(f32) + xr[1, 0].astype(f32)
         cps[0, 1, 0].wait_recv()
         cps[0, 1, 1].wait_recv()
-        p[:, 0:W] = scale * (p[:, 0:W] + ar[...])
-        p[:, W:E] = scale * (p[:, W:E] + ar_half[...].astype(f32))
+        p[:, 0:W] += ar[...]
+        p[:, W:E] += ar_half[...].astype(f32)
         store = pltpu.make_async_copy(p, out, sem)
         store.start()
         return store
@@ -582,11 +582,9 @@
     for cp in sc2_out:
         cp.wait()
     gs_ref[0, 0] = jnp.sum(sum(SR2[n] for n in range(8))) / c2
-    store_i = finish(ri, MS.at[0], XR, AR, ARH, gi_hbm, LS.at[0])
-    store_t = finish(rt, ltext(0), XRT, ART, ARHT, gt_hbm, LS.at[1])
-
-    for cp in rows_out + cols_out:
-        cp.wait_send()
+    store_i = finish(ri, MS.at[0], XR, AR, ARH, out_hbm.at[0], LS.at[0])
+    store_t = finish(rt, ltext(0), XRT, ART, ARHT, out_hbm.at[1], LS.at[1])
+
     for cps in (ri, rt):
         for (ring, pair, _), cp in cps.items():
             if ring == 0 or pair == 0:
@@ -599,15 +597,14 @@
     f32, bf16 = jnp.float32, jnp.bfloat16
     any_space = pl.BlockSpec(memory_space=pl.ANY)
     smem = pl.BlockSpec(memory_space=pltpu.SMEM)
-    grad_image, grad_text, grad_scale = pl.pallas_call(
+    grads, grad_scale = pl.pallas_call(
         kernel,
         out_shape=(
-            jax.ShapeDtypeStruct((B, E), f32),
-            jax.ShapeDtypeStruct((B, E), f32),
+            jax.ShapeDtypeStruct((2, B, E), f32),
             jax.ShapeDtypeStruct((1, 1), f32),
         ),
         in_specs=[smem, any_space, any_space],
-        out_specs=(any_space, any_space, smem),
+        out_specs=(any_space, smem),
         scratch_shapes=[
             pltpu.VMEM((16 * B, E), bf16),
             pltpu.VMEM((8 * B, E), bf16),
@@ -653,7 +650,7 @@
         ),
         cost_estimate=pl.CostEstimate(flops=6 * 4096 * 2048 * 512, bytes_accessed=4 << 20, transcendentals=4 * 4096 * 2048),
     )(logit_scale.reshape(1), image_embeds, text_embeds)
-    return grad_image, grad_text, grad_scale.reshape(())
+    return logit_scale * grads[0], logit_scale * grads[1], grad_scale.reshape(())
 
 
 def solution(mesh):

time: 101 us -> 102 us (level)
  local copies, waits for them, and re-layouts: 2.72 us -> 0 us
  other arithmetic: 0 us -> 2.26 us
  Pallas kernels: 94.6 us -> 96.3 us
    unnamed x4 -> x0, local copies, waits for them, and re-layouts: 2.72 us -> none
    mul x0 -> x1, other arithmetic: none -> 2.26 us  [on_device(): logit_scale * grads[1]]
    pallas_call x1, Pallas kernels: 94.6 us -> 96.3 us  [on_device(): pl.pallas_call(kernel, out_shape=(jax.ShapeDtypeStruct((2, B, E), f32), j...]
where the time goes in v4:
time: 102 us
  Pallas kernels  96.3 us (94%)
  between operations  3.05 us (3%)
  other arithmetic  2.26 us (2%)
    pallas_call x1, Pallas kernels, on_device(): pl.pallas_call(kernel, out_shape=(jax.ShapeDtypeStruct((2, B, E), f32), j...  96.3 us
    mul x1, other arithmetic, on_device(): logit_scale * grads[1]  2.26 us

profile of v4, /device:TPU:0, one launch (start us, length us, event | category | flops | bytes accessed | tf_op | source)
XLA Modules:
  0.0 101.6 jit_solution(10033931703939659552)
XLA Ops:
  1.3 96.3 %shard_map.58 = (f32[2,256,512]{2,1,0:T(8,128)}, f32[1,1]{1,0:T(1,128)}) custom-call(f32[1]{0:T(128)} %bitcast.6.scale_ref, f32[256,512]{1,0:T(8,128)} %img_hbm.1, f32[256,512]{1,0:T(8,128)} %txt_hbm.1), custom_call_target="tpu_custom_call" | custom-call | flops 25769803776 | bytes 4194304 | tf_op jit(solution)/shard_map/pallas_call | solution.py:600
  97.6 2.3 %multiply_bitcast_fusion = (f32[256,512]{1,0:T(8,128)}, f32[256,512]{1,0:T(8,128)}) fusion(f32[2,256,512]{2,1,0:T(8,128)} %get-tuple-element.5, f32[]{:T(128)} %copy.7), kind=kLoop, calls=%fused_computation | loop fusion | flops 262144 | bytes 2097156 | tf_op jit(solution)/shard_map/mul | solution.py:653
